TPU v7x, 32 devices: a whole 2x2x4 slice. The times are simulated.
32 devices in a mesh: sec: 4 (over x, core), dom: 8 (over z, y).
Axes of the slice: x: 2, y: 2, z: 4, core: 2. Of those that a mesh axis runs over, the one named last changes fastest.
Arguments:
- actuator_fields: float32 [16, 64, 4096], P(None, 'dom', 'sec'), may hold values from -6 to 6
- sensor_fields: float32 [8, 64, 4096], P(None, 'dom', 'sec'), may hold values from -6 to 6
- region_ids: int32 [64, 4096], P('dom', 'sec'), may hold values from 0 to 15
- stiffness_table: float32 [16], replicated, may hold values from 1 to 4
- density_table: float32 [16], replicated, may hold values from 1 to 2
- supported: int32 [10, 8, 32], P(None, 'dom', 'sec'), may hold values 0 or 1
Outputs:
- final_position: float32 [24, 64, 4096], P(None, 'dom', 'sec')
- cross: float32 [160, 80], P('sec')
All inputs are finite; a program needn't handle non-finite values. No bound on the sum of `supported` on one device may be relied on, other than what follows from the above.
Results may differ from a plain program's by a relative error of at most 0.0028.
Values sent between devices are 32-bit elements; how exact they have to be, the bound alone decides.
A program may use at most 64 MiB of HBM per device.

v0:
```python
import math

import jax
import jax.numpy as jnp
from jax import lax
from jax.sharding import PartitionSpec as P

TILE_Y = 128
ACT = 16
SNAPS = 10


def padded_2(cells, sides, width):
    for axis, dim in sides:
        count = lax.axis_size(axis)
        ends = count - 1
        head = lax.slice_in_dim(cells, 0, width, axis=dim)
        tail = lax.slice_in_dim(cells, cells.shape[dim] - width, cells.shape[dim], axis=dim)
        cells = jnp.concatenate(
            [
                lax.ppermute(tail, axis, [(i, (i + 1) % count) for i in range(ends)]),
                cells,
                lax.ppermute(head, axis, [((i + 1) % count, i) for i in range(ends)]),
            ],
            axis=dim,
        )
    return cells


def divergence(padded, stiff_pad):
    rows = padded.shape[-2] - 2
    cols = padded.shape[-1] - 2
    centre = padded[..., 1 : 1 + rows, 1 : 1 + cols]
    stiff_centre = stiff_pad[1 : 1 + rows, 1 : 1 + cols]
    total = jnp.zeros_like(centre)
    for first, second in ((0, 1), (2, 1), (1, 0), (1, 2)):
        nearby = padded[..., first : first + rows, second : second + cols]
        stiff_near = stiff_pad[first : first + rows, second : second + cols]
        total = total + 0.5 * (stiff_centre + stiff_near) * (nearby - centre)
    return total


def lookup(region_ids, table):
    labels = jnp.arange(table.shape[0], dtype=jnp.int32)
    match = (region_ids[None, :, :] == labels[:, None, None]).astype(jnp.float32)
    return jnp.sum(match * table[:, None, None], axis=0)


def body(actuator_fields, sensor_fields, region_ids, stiffness_table, density_table, supported):
    stiffness = lookup(region_ids, stiffness_table)
    inv_mass = 1.0 / lookup(region_ids, density_table)
    depth = 2
    stiff_pad, mass_pad = (
        padded_2(stiffness, (("sec", 1), ("dom", 0)), depth),
        padded_2(inv_mass, (("sec", 1), ("dom", 0)), depth),
    )
    velocity = jnp.concatenate([actuator_fields, sensor_fields], 0) * inv_mass
    position = jnp.zeros_like(velocity)
    count = velocity.shape[0]
    rows, cols = stiffness.shape
    frames = jnp.zeros((count, SNAPS, 2, rows, cols), jnp.bfloat16)

    def advance(position, velocity):
        pos_pad, vel_pad = (
            padded_2(position, (("sec", 2), ("dom", 1)), 2),
            padded_2(velocity, (("sec", 2), ("dom", 1)), 2),
        )
        vel_ext = vel_pad[:, 1:-1, 1:-1] + 0.35 * mass_pad[1:-1, 1:-1] * divergence(
            pos_pad, stiff_pad
        )
        pos_ext = pos_pad[:, 1:-1, 1:-1] + 0.35 * vel_ext
        velocity = vel_ext[:, 1:-1, 1:-1] + 0.35 * inv_mass * divergence(
            pos_ext, stiff_pad[1:-1, 1:-1]
        )
        return (pos_ext[:, 1:-1, 1:-1] + 0.35 * velocity, velocity)

    def pair_step(index, carry):
        position, velocity, frames = carry
        position, velocity = advance(position, velocity)
        mask_row = lax.dynamic_index_in_dim(supported, index, 0, keepdims=False)
        cells = jnp.repeat(mask_row, TILE_Y, axis=1).astype(jnp.float32)
        frame = jnp.stack([position * cells, velocity * cells], 1).astype(jnp.bfloat16)
        frames = lax.dynamic_update_slice_in_dim(frames, frame[:, None], index, 1)
        return (position, velocity, frames)

    position, velocity, frames = lax.fori_loop(0, SNAPS, pair_step, (position, velocity, frames))
    flat_frames = frames.reshape(count * SNAPS, 2 * rows * cols)
    primal = flat_frames[: ACT * SNAPS]
    adjoint = flat_frames[ACT * SNAPS :]
    local = lax.dot_general(
        primal, adjoint, (((1,), (1,)), ((), ())), preferred_element_type=jnp.float32
    )
    factor = 1.0 / math.sqrt(rows * cols * lax.axis_size("sec") * lax.axis_size("dom"))
    total = lax.psum(local, ("sec", "dom"))
    share = local.shape[0] // lax.axis_size("sec")
    block = lax.dynamic_slice_in_dim(total, lax.axis_index("sec") * share, share, 0)
    return (position, block * factor)


def solution(mesh):
    in_specs = (
        P(None, "dom", "sec"),
        P(None, "dom", "sec"),
        P("dom", "sec"),
        P(),
        P(),
        P(None, "dom", "sec"),
    )
    out_specs = (P(None, "dom", "sec"), P("sec", None))
    return jax.shard_map(body, mesh=mesh, in_specs=in_specs, out_specs=out_specs, check_vma=False)
```

profile of v0, /device:TPU:0, one launch (start us, length us, event | category | flops | bytes accessed | tf_op | source)
XLA Modules:
  0.0 566.6 jit_solution(8961645408353022031)
XLA Ops:
  29.3 464.0 %while.20 = (s32[]{:T(128)}, f32[24,8,1024]{2,1,0:T(8,128)S(1)}, f32[24,8,1024]{2,1,0:T(8,128)S(1)}, bf16[24,10,2,8,1024]{4,3,0,2,1:T(8,128)(2,1)}, f32[12,1028]...) while((s32[]{:T(128)}, f32[24,8,1024]{2,1,0:T(8,128)S(1)}, ...), condition=%wide.region_3.4_spmd.clone, body=%wide.region_2.3_spmd.clone.sunk | while | flops 10867983 | bytes 33129760 | solution.py:86
  33.6 6.0 %collective-permute-start.4 = (f32[24,8,2]{2,1,0:T(8,128)S(1)}, f32[24,8,2]{2,1,0:T(8,128)S(1)}, u32[]{:S(2)}, u32[]{:S(2)}) collective-permute-start(f32[24,8,2]{2,1,0:T(8,128)S(1)} %get-tuple-element.515), channel_id=1, source_target_pairs={{0,8},{8,16},{16,24},{1,9},{9,17},{17,25},{2,10},{10,18},{18,26},{... | collective-permute-start | bytes 4616 | tf_op jit(solution)/shard_map/while/body/eval_jaxpr/ppermute | solution.py:21
  46.9 5.5 collective-permute-start.3
  56.0 5.4 collective-permute-start.7
  64.7 6.7 %collective-permute-done.7 = f32[24,2,1028]{2,1,0:T(2,128)S(1)} collective-permute-done((f32[24,2,1028]{2,1,0:T(2,128)S(1)}, f32[24,2,1028]{2,1,0:T(2,128)S(1)}, u32[]{:S(2)}, u32[]{:S(2)}) %collective-permute-start.7) | collective-permute-done | bytes 197408 | tf_op jit(solution)/shard_map/while/body/eval_jaxpr/ppermute | solution.py:21
  102.2 5.4 collective-permute-start.7
  110.9 6.7 %collective-permute-done.7 = f32[24,2,1028]{2,1,0:T(2,128)S(1)} collective-permute-done((f32[24,2,1028]{2,1,0:T(2,128)S(1)}, f32[24,2,1028]{2,1,0:T(2,128)S(1)}, u32[]{:S(2)}, u32[]{:S(2)}) %collective-permute-start.7) | collective-permute-done | bytes 197408 | tf_op jit(solution)/shard_map/while/body/eval_jaxpr/ppermute | solution.py:21
  148.4 5.4 collective-permute-start.7
  157.1 6.7 %collective-permute-done.7 = f32[24,2,1028]{2,1,0:T(2,128)S(1)} collective-permute-done((f32[24,2,1028]{2,1,0:T(2,128)S(1)}, f32[24,2,1028]{2,1,0:T(2,128)S(1)}, u32[]{:S(2)}, u32[]{:S(2)}) %collective-permute-start.7) | collective-permute-done | bytes 197408 | tf_op jit(solution)/shard_map/while/body/eval_jaxpr/ppermute | solution.py:21
  194.6 5.4 collective-permute-start.7
  203.3 6.7 %collective-permute-done.7 = f32[24,2,1028]{2,1,0:T(2,128)S(1)} collective-permute-done((f32[24,2,1028]{2,1,0:T(2,128)S(1)}, f32[24,2,1028]{2,1,0:T(2,128)S(1)}, u32[]{:S(2)}, u32[]{:S(2)}) %collective-permute-start.7) | collective-permute-done | bytes 197408 | tf_op jit(solution)/shard_map/while/body/eval_jaxpr/ppermute | solution.py:21
  240.8 5.4 collective-permute-start.7
  249.5 6.7 %collective-permute-done.7 = f32[24,2,1028]{2,1,0:T(2,128)S(1)} collective-permute-done((f32[24,2,1028]{2,1,0:T(2,128)S(1)}, f32[24,2,1028]{2,1,0:T(2,128)S(1)}, u32[]{:S(2)}, u32[]{:S(2)}) %collective-permute-start.7) | collective-permute-done | bytes 197408 | tf_op jit(solution)/shard_map/while/body/eval_jaxpr/ppermute | solution.py:21
  287.0 5.4 collective-permute-start.7
  295.7 6.7 %collective-permute-done.7 = f32[24,2,1028]{2,1,0:T(2,128)S(1)} collective-permute-done((f32[24,2,1028]{2,1,0:T(2,128)S(1)}, f32[24,2,1028]{2,1,0:T(2,128)S(1)}, u32[]{:S(2)}, u32[]{:S(2)}) %collective-permute-start.7) | collective-permute-done | bytes 197408 | tf_op jit(solution)/shard_map/while/body/eval_jaxpr/ppermute | solution.py:21
  333.2 5.4 collective-permute-start.7
  341.9 6.7 %collective-permute-done.7 = f32[24,2,1028]{2,1,0:T(2,128)S(1)} collective-permute-done((f32[24,2,1028]{2,1,0:T(2,128)S(1)}, f32[24,2,1028]{2,1,0:T(2,128)S(1)}, u32[]{:S(2)}, u32[]{:S(2)}) %collective-permute-start.7) | collective-permute-done | bytes 197408 | tf_op jit(solution)/shard_map/while/body/eval_jaxpr/ppermute | solution.py:21
  388.1 6.7 %collective-permute-done.7 = f32[24,2,1028]{2,1,0:T(2,128)S(1)} collective-permute-done((f32[24,2,1028]{2,1,0:T(2,128)S(1)}, f32[24,2,1028]{2,1,0:T(2,128)S(1)}, u32[]{:S(2)}, u32[]{:S(2)}) %collective-permute-start.7) | collective-permute-done | bytes 197408 | tf_op jit(solution)/shard_map/while/body/eval_jaxpr/ppermute | solution.py:21
  425.6 5.4 collective-permute-start.7
  434.3 6.7 %collective-permute-done.7 = f32[24,2,1028]{2,1,0:T(2,128)S(1)} collective-permute-done((f32[24,2,1028]{2,1,0:T(2,128)S(1)}, f32[24,2,1028]{2,1,0:T(2,128)S(1)}, u32[]{:S(2)}, u32[]{:S(2)}) %collective-permute-start.7) | collective-permute-done | bytes 197408 | tf_op jit(solution)/shard_map/while/body/eval_jaxpr/ppermute | solution.py:21
  471.8 5.4 collective-permute-start.7
  480.5 6.7 %collective-permute-done.7 = f32[24,2,1028]{2,1,0:T(2,128)S(1)} collective-permute-done((f32[24,2,1028]{2,1,0:T(2,128)S(1)}, f32[24,2,1028]{2,1,0:T(2,128)S(1)}, u32[]{:S(2)}, u32[]{:S(2)}) %collective-permute-start.7) | collective-permute-done | bytes 197408 | tf_op jit(solution)/shard_map/while/body/eval_jaxpr/ppermute | solution.py:21
  503.9 9.1 %slice.350 = bf16[160,16384]{1,0:T(8,128)(2,1)} reshape(bf16[16,10,2,8,1024]{4,3,2,1,0:T(8,128)(2,1)} %copy.13) | data formatting | bytes 10485760 | tf_op jit(solution)/shard_map/slice | solution.py:88
  522.8 43.2 %psum.7 = f32[160,80]{1,0:T(8,128)S(1)} all-reduce(f32[160,80]{1,0:T(8,128)S(1)} %fusion.36), channel_id=1, replica_groups=mesh['sec'=4,'dom'=8] {'sec','dom'}, use_global_device_ids=true, to_apply=%region_4.5 | all-reduce | flops 12800 | bytes 102400 | tf_op jit(solution)/shard_map/psum | solution.py:94
  (902 shorter events, 380.5 us)
Async XLA Ops:
  33.6 18.7 %collective-permute-start.4 = (f32[24,8,2]{2,1,0:T(8,128)S(1)}, f32[24,8,2]{2,1,0:T(8,128)S(1)}, u32[]{:S(2)}, u32[]{:S(2)}) collective-permute-start(f32[24,8,2]{2,1,0:T(8,128)S(1)} %get-tuple-element.515), channel_id=1, source_target_pairs={{0,8},{8,16},{16,24},{1,9},{9,17},{17,25},{2,10},{10,18},{18,26},{... | collective-permute-start | bytes 4616 | tf_op jit(solution)/shard_map/while/body/eval_jaxpr/ppermute | solution.py:21
  45.6 15.9 %collective-permute-start.2 = (f32[24,2,1028]{2,1,0:T(2,128)}, f32[24,2,1028]{2,1,0:T(2,128)S(1)}, u32[]{:S(2)}, u32[]{:S(2)}) collective-permute-start(f32[24,2,1028]{2,1,0:T(2,128)} %get-tuple-element.509), channel_id=1, source_target_pairs={{1,0},{2,1},{3,2},{4,3},{5,4},{6,5},{7,6},{9,8},{10,9},{11,10},{12... | collective-permute-start | bytes 592136 | tf_op jit(solution)/shard_map/while/body/eval_jaxpr/ppermute | solution.py:23
  56.0 15.4 %collective-permute-start.7 = (f32[24,2,1028]{2,1,0:T(2,128)S(1)}, f32[24,2,1028]{2,1,0:T(2,128)S(1)}, u32[]{:S(2)}, u32[]{:S(2)}) collective-permute-start(f32[24,2,1028]{2,1,0:T(2,128)S(1)} %get-tuple-element.518), channel_id=1, source_target_pairs={{0,1},{1,2},{2,3},{3,4},{4,5},{5,6},{6,7},{8,9},{9,10},{10,11},{11... | collective-permute-start | bytes 592136 | tf_op jit(solution)/shard_map/while/body/eval_jaxpr/ppermute | solution.py:21
  81.4 17.2 %collective-permute-start.4 = (f32[24,8,2]{2,1,0:T(8,128)S(1)}, f32[24,8,2]{2,1,0:T(8,128)S(1)}, u32[]{:S(2)}, u32[]{:S(2)}) collective-permute-start(f32[24,8,2]{2,1,0:T(8,128)S(1)} %get-tuple-element.515), channel_id=1, source_target_pairs={{0,8},{8,16},{16,24},{1,9},{9,17},{17,25},{2,10},{10,18},{18,26},{... | collective-permute-start | bytes 4616 | tf_op jit(solution)/shard_map/while/body/eval_jaxpr/ppermute | solution.py:21
  92.2 15.5 %collective-permute-start.2 = (f32[24,2,1028]{2,1,0:T(2,128)}, f32[24,2,1028]{2,1,0:T(2,128)S(1)}, u32[]{:S(2)}, u32[]{:S(2)}) collective-permute-start(f32[24,2,1028]{2,1,0:T(2,128)} %get-tuple-element.509), channel_id=1, source_target_pairs={{1,0},{2,1},{3,2},{4,3},{5,4},{6,5},{7,6},{9,8},{10,9},{11,10},{12... | collective-permute-start | bytes 592136 | tf_op jit(solution)/shard_map/while/body/eval_jaxpr/ppermute | solution.py:23
  102.2 15.4 %collective-permute-start.7 = (f32[24,2,1028]{2,1,0:T(2,128)S(1)}, f32[24,2,1028]{2,1,0:T(2,128)S(1)}, u32[]{:S(2)}, u32[]{:S(2)}) collective-permute-start(f32[24,2,1028]{2,1,0:T(2,128)S(1)} %get-tuple-element.518), channel_id=1, source_target_pairs={{0,1},{1,2},{2,3},{3,4},{4,5},{5,6},{6,7},{8,9},{9,10},{10,11},{11... | collective-permute-start | bytes 592136 | tf_op jit(solution)/shard_map/while/body/eval_jaxpr/ppermute | solution.py:21
  127.6 17.2 %collective-permute-start.4 = (f32[24,8,2]{2,1,0:T(8,128)S(1)}, f32[24,8,2]{2,1,0:T(8,128)S(1)}, u32[]{:S(2)}, u32[]{:S(2)}) collective-permute-start(f32[24,8,2]{2,1,0:T(8,128)S(1)} %get-tuple-element.515), channel_id=1, source_target_pairs={{0,8},{8,16},{16,24},{1,9},{9,17},{17,25},{2,10},{10,18},{18,26},{... | collective-permute-start | bytes 4616 | tf_op jit(solution)/shard_map/while/body/eval_jaxpr/ppermute | solution.py:21
  138.4 15.5 %collective-permute-start.2 = (f32[24,2,1028]{2,1,0:T(2,128)}, f32[24,2,1028]{2,1,0:T(2,128)S(1)}, u32[]{:S(2)}, u32[]{:S(2)}) collective-permute-start(f32[24,2,1028]{2,1,0:T(2,128)} %get-tuple-element.509), channel_id=1, source_target_pairs={{1,0},{2,1},{3,2},{4,3},{5,4},{6,5},{7,6},{9,8},{10,9},{11,10},{12... | collective-permute-start | bytes 592136 | tf_op jit(solution)/shard_map/while/body/eval_jaxpr/ppermute | solution.py:23
  148.4 15.4 %collective-permute-start.7 = (f32[24,2,1028]{2,1,0:T(2,128)S(1)}, f32[24,2,1028]{2,1,0:T(2,128)S(1)}, u32[]{:S(2)}, u32[]{:S(2)}) collective-permute-start(f32[24,2,1028]{2,1,0:T(2,128)S(1)} %get-tuple-element.518), channel_id=1, source_target_pairs={{0,1},{1,2},{2,3},{3,4},{4,5},{5,6},{6,7},{8,9},{9,10},{10,11},{11... | collective-permute-start | bytes 592136 | tf_op jit(solution)/shard_map/while/body/eval_jaxpr/ppermute | solution.py:21
  173.8 17.2 %collective-permute-start.4 = (f32[24,8,2]{2,1,0:T(8,128)S(1)}, f32[24,8,2]{2,1,0:T(8,128)S(1)}, u32[]{:S(2)}, u32[]{:S(2)}) collective-permute-start(f32[24,8,2]{2,1,0:T(8,128)S(1)} %get-tuple-element.515), channel_id=1, source_target_pairs={{0,8},{8,16},{16,24},{1,9},{9,17},{17,25},{2,10},{10,18},{18,26},{... | collective-permute-start | bytes 4616 | tf_op jit(solution)/shard_map/while/body/eval_jaxpr/ppermute | solution.py:21
  184.6 15.5 %collective-permute-start.2 = (f32[24,2,1028]{2,1,0:T(2,128)}, f32[24,2,1028]{2,1,0:T(2,128)S(1)}, u32[]{:S(2)}, u32[]{:S(2)}) collective-permute-start(f32[24,2,1028]{2,1,0:T(2,128)} %get-tuple-element.509), channel_id=1, source_target_pairs={{1,0},{2,1},{3,2},{4,3},{5,4},{6,5},{7,6},{9,8},{10,9},{11,10},{12... | collective-permute-start | bytes 592136 | tf_op jit(solution)/shard_map/while/body/eval_jaxpr/ppermute | solution.py:23
  220.0 17.2 %collective-permute-start.4 = (f32[24,8,2]{2,1,0:T(8,128)S(1)}, f32[24,8,2]{2,1,0:T(8,128)S(1)}, u32[]{:S(2)}, u32[]{:S(2)}) collective-permute-start(f32[24,8,2]{2,1,0:T(8,128)S(1)} %get-tuple-element.515), channel_id=1, source_target_pairs={{0,8},{8,16},{16,24},{1,9},{9,17},{17,25},{2,10},{10,18},{18,26},{... | collective-permute-start | bytes 4616 | tf_op jit(solution)/shard_map/while/body/eval_jaxpr/ppermute | solution.py:21
  230.8 15.5 %collective-permute-start.2 = (f32[24,2,1028]{2,1,0:T(2,128)}, f32[24,2,1028]{2,1,0:T(2,128)S(1)}, u32[]{:S(2)}, u32[]{:S(2)}) collective-permute-start(f32[24,2,1028]{2,1,0:T(2,128)} %get-tuple-element.509), channel_id=1, source_target_pairs={{1,0},{2,1},{3,2},{4,3},{5,4},{6,5},{7,6},{9,8},{10,9},{11,10},{12... | collective-permute-start | bytes 592136 | tf_op jit(solution)/shard_map/while/body/eval_jaxpr/ppermute | solution.py:23
  266.2 17.2 %collective-permute-start.4 = (f32[24,8,2]{2,1,0:T(8,128)S(1)}, f32[24,8,2]{2,1,0:T(8,128)S(1)}, u32[]{:S(2)}, u32[]{:S(2)}) collective-permute-start(f32[24,8,2]{2,1,0:T(8,128)S(1)} %get-tuple-element.515), channel_id=1, source_target_pairs={{0,8},{8,16},{16,24},{1,9},{9,17},{17,25},{2,10},{10,18},{18,26},{... | collective-permute-start | bytes 4616 | tf_op jit(solution)/shard_map/while/body/eval_jaxpr/ppermute | solution.py:21
  277.0 15.5 %collective-permute-start.2 = (f32[24,2,1028]{2,1,0:T(2,128)}, f32[24,2,1028]{2,1,0:T(2,128)S(1)}, u32[]{:S(2)}, u32[]{:S(2)}) collective-permute-start(f32[24,2,1028]{2,1,0:T(2,128)} %get-tuple-element.509), channel_id=1, source_target_pairs={{1,0},{2,1},{3,2},{4,3},{5,4},{6,5},{7,6},{9,8},{10,9},{11,10},{12... | collective-permute-start | bytes 592136 | tf_op jit(solution)/shard_map/while/body/eval_jaxpr/ppermute | solution.py:23
  312.4 17.2 %collective-permute-start.4 = (f32[24,8,2]{2,1,0:T(8,128)S(1)}, f32[24,8,2]{2,1,0:T(8,128)S(1)}, u32[]{:S(2)}, u32[]{:S(2)}) collective-permute-start(f32[24,8,2]{2,1,0:T(8,128)S(1)} %get-tuple-element.515), channel_id=1, source_target_pairs={{0,8},{8,16},{16,24},{1,9},{9,17},{17,25},{2,10},{10,18},{18,26},{... | collective-permute-start | bytes 4616 | tf_op jit(solution)/shard_map/while/body/eval_jaxpr/ppermute | solution.py:21
  323.2 15.5 %collective-permute-start.2 = (f32[24,2,1028]{2,1,0:T(2,128)}, f32[24,2,1028]{2,1,0:T(2,128)S(1)}, u32[]{:S(2)}, u32[]{:S(2)}) collective-permute-start(f32[24,2,1028]{2,1,0:T(2,128)} %get-tuple-element.509), channel_id=1, source_target_pairs={{1,0},{2,1},{3,2},{4,3},{5,4},{6,5},{7,6},{9,8},{10,9},{11,10},{12... | collective-permute-start | bytes 592136 | tf_op jit(solution)/shard_map/while/body/eval_jaxpr/ppermute | solution.py:23
  358.6 17.2 %collective-permute-start.4 = (f32[24,8,2]{2,1,0:T(8,128)S(1)}, f32[24,8,2]{2,1,0:T(8,128)S(1)}, u32[]{:S(2)}, u32[]{:S(2)}) collective-permute-start(f32[24,8,2]{2,1,0:T(8,128)S(1)} %get-tuple-element.515), channel_id=1, source_target_pairs={{0,8},{8,16},{16,24},{1,9},{9,17},{17,25},{2,10},{10,18},{18,26},{... | collective-permute-start | bytes 4616 | tf_op jit(solution)/shard_map/while/body/eval_jaxpr/ppermute | solution.py:21
  369.4 15.5 %collective-permute-start.2 = (f32[24,2,1028]{2,1,0:T(2,128)}, f32[24,2,1028]{2,1,0:T(2,128)S(1)}, u32[]{:S(2)}, u32[]{:S(2)}) collective-permute-start(f32[24,2,1028]{2,1,0:T(2,128)} %get-tuple-element.509), channel_id=1, source_target_pairs={{1,0},{2,1},{3,2},{4,3},{5,4},{6,5},{7,6},{9,8},{10,9},{11,10},{12... | collective-permute-start | bytes 592136 | tf_op jit(solution)/shard_map/while/body/eval_jaxpr/ppermute | solution.py:23
  404.8 17.2 %collective-permute-start.4 = (f32[24,8,2]{2,1,0:T(8,128)S(1)}, f32[24,8,2]{2,1,0:T(8,128)S(1)}, u32[]{:S(2)}, u32[]{:S(2)}) collective-permute-start(f32[24,8,2]{2,1,0:T(8,128)S(1)} %get-tuple-element.515), channel_id=1, source_target_pairs={{0,8},{8,16},{16,24},{1,9},{9,17},{17,25},{2,10},{10,18},{18,26},{... | collective-permute-start | bytes 4616 | tf_op jit(solution)/shard_map/while/body/eval_jaxpr/ppermute | solution.py:21
  415.6 15.5 %collective-permute-start.2 = (f32[24,2,1028]{2,1,0:T(2,128)}, f32[24,2,1028]{2,1,0:T(2,128)S(1)}, u32[]{:S(2)}, u32[]{:S(2)}) collective-permute-start(f32[24,2,1028]{2,1,0:T(2,128)} %get-tuple-element.509), channel_id=1, source_target_pairs={{1,0},{2,1},{3,2},{4,3},{5,4},{6,5},{7,6},{9,8},{10,9},{11,10},{12... | collective-permute-start | bytes 592136 | tf_op jit(solution)/shard_map/while/body/eval_jaxpr/ppermute | solution.py:23
  451.0 17.2 %collective-permute-start.4 = (f32[24,8,2]{2,1,0:T(8,128)S(1)}, f32[24,8,2]{2,1,0:T(8,128)S(1)}, u32[]{:S(2)}, u32[]{:S(2)}) collective-permute-start(f32[24,8,2]{2,1,0:T(8,128)S(1)} %get-tuple-element.515), channel_id=1, source_target_pairs={{0,8},{8,16},{16,24},{1,9},{9,17},{17,25},{2,10},{10,18},{18,26},{... | collective-permute-start | bytes 4616 | tf_op jit(solution)/shard_map/while/body/eval_jaxpr/ppermute | solution.py:21
  461.8 15.5 %collective-permute-start.2 = (f32[24,2,1028]{2,1,0:T(2,128)}, f32[24,2,1028]{2,1,0:T(2,128)S(1)}, u32[]{:S(2)}, u32[]{:S(2)}) collective-permute-start(f32[24,2,1028]{2,1,0:T(2,128)} %get-tuple-element.509), channel_id=1, source_target_pairs={{1,0},{2,1},{3,2},{4,3},{5,4},{6,5},{7,6},{9,8},{10,9},{11,10},{12... | collective-permute-start | bytes 592136 | tf_op jit(solution)/shard_map/while/body/eval_jaxpr/ppermute | solution.py:23
  471.8 15.4 %collective-permute-start.7 = (f32[24,2,1028]{2,1,0:T(2,128)S(1)}, f32[24,2,1028]{2,1,0:T(2,128)S(1)}, u32[]{:S(2)}, u32[]{:S(2)}) collective-permute-start(f32[24,2,1028]{2,1,0:T(2,128)S(1)} %get-tuple-element.518), channel_id=1, source_target_pairs={{0,1},{1,2},{2,3},{3,4},{4,5},{5,6},{6,7},{8,9},{9,10},{10,11},{11... | collective-permute-start | bytes 592136 | tf_op jit(solution)/shard_map/while/body/eval_jaxpr/ppermute | solution.py:21
  (326 other events, 2933.0 us)
where the time goes:
time: 571 us; the launch traced here: 567 us
  starting transfers between devices  251 us (44%)
  waiting for transfers between devices  99.8 us (17%)
  other arithmetic  91.4 us (16%)
  local copies, waits for them, and re-layouts  71.5 us (13%)
  blocking collectives  43.2 us (8%)
    ppermute x44, starting transfers between devices, padded_2(): lax.ppermute(tail, axis, [(i, (i + 1) % count) for i in range(ends)])  193 us
    ppermute x44, waiting for transfers between devices, padded_2(): lax.ppermute(tail, axis, [(i, (i + 1) % count) for i in range(ends)])  71.7 us
    ppermute x44, starting transfers between devices, padded_2(): lax.ppermute(head, axis, [((i + 1) % count, i) for i in range(ends)])  58.1 us
    psum x1, blocking collectives, body(): total = lax.psum(local, ('sec', 'dom'))  43.2 us
    add x10, other arithmetic, advance(): pos_ext = pos_pad[:, 1:-1, 1:-1] + 0.35 * vel_ext  36.7 us
    ppermute x44, waiting for transfers between devices, padded_2(): lax.ppermute(head, axis, [((i + 1) % count, i) for i in range(ends)])  28.1 us
    concatenate x22, local copies, waits for them, and re-layouts, padded_2(): jnp.concatenate([lax.ppermute(tail, axis, [(i, (i + 1) % count) for i in...  19.1 us
    mul x40, other arithmetic, divergence(): total = total + 0.5 * (stiff_centre + stiff_near) * (nearby - centre)  18.9 us
  transfers between devices with their start and end apart: 88, of which 31 were waited for; matrix products, arithmetic and copies ran while one was open for 12% of the time, Pallas kernels for 0%

commit v1 on v0

--- a/solution.py
+++ b/solution.py
@@ -1,8 +1,11 @@
+import functools
 import math
 
 import jax
 import jax.numpy as jnp
 from jax import lax
+from jax.experimental import pallas as pl
+from jax.experimental.pallas import tpu as pltpu
 from jax.sharding import PartitionSpec as P
 
 TILE_Y = 128
@@ -97,6 +100,289 @@
     return (position, block * factor)
 
 
+HALO = 24
+LANES = 128
+SUB = 8
+MESH = pl.DeviceIdType.MESH
+
+
+def wave_kernel(dims, act_ref, sens_ref, aux_ref, out_ref, part_ref,
+                recv, field, coef, masks, pos_a, pos_b, vel, frames, back,
+                in_send, in_recv, halo_send, halo_recv, out_send, out_recv):
+    n_sec, n_dom, n_act, n_sens, steps = dims
+    sec = lax.axis_index("sec")
+    dom = lax.axis_index("dom")
+    place = sec * n_dom + dom
+    total = n_sec * n_dom
+    n_resp = n_act + n_sens
+    pairs = n_resp // 2
+    act_pairs = n_act // 2
+    sens_pairs = n_sens // 2
+    core = LANES
+    ext = core + 2 * HALO
+    left = lax.rem(place + total - 1, total)
+    right = lax.rem(place + 1, total)
+    left_id = (left // n_dom, lax.rem(left, n_dom))
+    right_id = (right // n_dom, lax.rem(right, n_dom))
+
+    barrier = pltpu.get_barrier_semaphore()
+    for off in range(1, n_dom):
+        pl.semaphore_signal(barrier, inc=1, device_id=(sec, lax.rem(dom + off, n_dom)), device_id_type=MESH)
+    pl.semaphore_signal(barrier, inc=1, device_id=left_id, device_id_type=MESH)
+    pl.semaphore_signal(barrier, inc=1, device_id=right_id, device_id_type=MESH)
+    pl.semaphore_wait(barrier, n_dom + 1)
+
+    my_rows = pl.ds(pl.multiple_of(dom * SUB, SUB), SUB)
+    my_cols = pl.ds(pl.multiple_of(dom * LANES, LANES), LANES)
+    groups = ((aux_ref, n_resp, 3), (act_ref, 0, n_act), (sens_ref, n_act, n_sens))
+    copies = []
+    for g, (src, first, count) in enumerate(groups):
+        for off in range(1, n_dom):
+            peer = lax.rem(dom + off, n_dom)
+            cols = pl.ds(pl.multiple_of(peer * LANES, LANES), LANES)
+            copy = pltpu.make_async_remote_copy(
+                src_ref=src.at[:, :, cols],
+                dst_ref=recv.at[pl.ds(first, count), my_rows, :],
+                send_sem=in_send.at[g, off - 1],
+                recv_sem=in_recv.at[g, off - 1],
+                device_id=(sec, peer),
+                device_id_type=MESH,
+            )
+            copy.start()
+            copies.append(copy)
+    for src, first, count in groups:
+        recv[pl.ds(first, count), my_rows, :] = src[:, :, my_cols]
+    for copy in copies:
+        copy.wait()
+
+    inner = pl.ds(HALO, core)
+
+    def flip(first, second):
+        return jnp.concatenate([recv[first], recv[second]], 0).T
+
+    for p in range(pairs):
+        if p < act_pairs:
+            first, second = p, p + act_pairs
+        else:
+            first = n_act + p - act_pairs
+            second = first + sens_pairs
+        field[p, inner, :] = flip(first, second)
+    field[pairs, inner, :] = flip(n_resp, n_resp)
+    field[pairs + 1, inner, :] = flip(n_resp + 1, n_resp + 1)
+    masks[...] = flip(n_resp + 2, n_resp + 2)[: masks.shape[0], :]
+
+    to_left = pltpu.make_async_remote_copy(
+        src_ref=field.at[:, pl.ds(HALO, HALO), :],
+        dst_ref=field.at[:, pl.ds(HALO + core, HALO), :],
+        send_sem=halo_send.at[0], recv_sem=halo_recv.at[0],
+        device_id=left_id, device_id_type=MESH,
+    )
+    to_right = pltpu.make_async_remote_copy(
+        src_ref=field.at[:, pl.ds(core, HALO), :],
+        dst_ref=field.at[:, pl.ds(0, HALO), :],
+        send_sem=halo_send.at[1], recv_sem=halo_recv.at[1],
+        device_id=right_id, device_id_type=MESH,
+    )
+    to_left.start()
+    to_right.start()
+    to_left.wait()
+    to_right.wait()
+
+    where = lax.broadcasted_iota(jnp.int32, (ext, LANES), 0)
+    lane = lax.broadcasted_iota(jnp.int32, (ext, LANES), 1)
+    height = LANES // 2
+    row = lax.rem(lane, height)
+    low = jnp.where(place == 0, HALO, 0)
+    high = jnp.where(place == total - 1, HALO + core, ext)
+    inside = (where >= low) & (where < high)
+    stiff = jnp.where(inside, field[pairs], 0.0)
+    mass = jnp.where(inside, field[pairs + 1], 0.0)
+    scale = (0.35 * 0.35 * 0.5) * mass
+    up_in = row > 0
+    down_in = row < height - 1
+    stiff_up = jnp.where(up_in, pltpu.roll(stiff, 1, 1), 0.0)
+    stiff_down = jnp.where(down_in, pltpu.roll(stiff, LANES - 1, 1), 0.0)
+    stiff_left = jnp.where(where > 0, pltpu.roll(stiff, 1, 0), 0.0)
+    stiff_right = jnp.where(where < ext - 1, pltpu.roll(stiff, ext - 1, 0), 0.0)
+    c_up = scale * (stiff + stiff_up)
+    c_down = scale * (stiff + stiff_down)
+    c_left = scale * (stiff + stiff_left)
+    c_right = scale * (stiff + stiff_right)
+    coef[0] = jnp.where(up_in, c_up, 0.0)
+    coef[1] = jnp.where(down_in, c_down, 0.0)
+    coef[2] = c_left
+    coef[3] = c_right
+    coef[4] = (c_up + c_down) + (c_left + c_right)
+    coef[5] = 0.35 * mass
+
+    n_tiles = ext // SUB
+    group = pos_a.shape[0]
+    snaps = steps // 2
+    height_rows = pairs * snaps
+
+    def advance(src, dst, store):
+        for t in range(n_tiles):
+            at = pl.ds(t * SUB, SUB)
+            cs = [coef[c, at, :] for c in range(5)]
+            for q in range(group):
+                centre = src[q, pl.ds(SUB + t * SUB, SUB), :]
+                before = src[q, pl.ds(SUB - 1 + t * SUB, SUB), :]
+                after = src[q, pl.ds(SUB + 1 + t * SUB, SUB), :]
+                gain = (cs[0] * pltpu.roll(centre, 1, 1) + cs[1] * pltpu.roll(centre, LANES - 1, 1)) + (
+                    cs[2] * before + cs[3] * after
+                )
+                new_vel = vel[q, at, :] + (gain - cs[4] * centre)
+                new_pos = centre + new_vel
+                vel[q, at, :] = new_vel
+                dst[q, pl.ds(SUB + t * SUB, SUB), :] = new_pos
+                if store is not None:
+                    store(q, t, new_pos, new_vel)
+
+    pad = jnp.zeros((group, SUB, LANES), jnp.float32)
+    for buf in (pos_a, pos_b):
+        buf[:, pl.ds(0, SUB), :] = pad
+        buf[:, pl.ds(SUB + ext, SUB), :] = pad
+
+    def run_group(index, carry):
+        for q in range(group):
+            here = index * group + q
+            vel[q] = jnp.where(inside, field[here] * coef[5], 0.0)
+            pos_a[q, pl.ds(SUB, ext), :] = jnp.zeros((ext, LANES), jnp.float32)
+
+        def pair_step(k, carry):
+            mask = jnp.broadcast_to(masks[pl.ds(k, 1), :], (SUB, LANES))
+            vmask = mask * (1.0 / 0.35)
+
+            def store(q, t, new_pos, new_vel):
+                if t * SUB < HALO or t * SUB >= HALO + core:
+                    return
+                y = t * SUB - HALO
+                base = y * height_rows + (index * group + q) * snaps + k
+                frames[pl.ds(base, SUB, stride=height_rows), :] = new_pos * mask
+                frames[pl.ds(base + core * height_rows, SUB, stride=height_rows), :] = new_vel * vmask
+
+            advance(pos_a, pos_b, None)
+            advance(pos_b, pos_a, store)
+            return carry
+
+        lax.fori_loop(0, snaps, pair_step, 0)
+        for q in range(group):
+            back[index * group + q] = pos_a[q, pl.ds(SUB + HALO, core), :].T
+        return carry
+
+    lax.fori_loop(0, pairs // group, run_group, 0)
+
+    sends = []
+    parts = ((0, act_pairs, 0), (act_pairs, sens_pairs, n_act))
+    for g, (first_pair, count, first) in enumerate(parts):
+        for half in range(2):
+            for off in range(1, n_dom):
+                peer = lax.rem(dom + off, n_dom)
+                rows = pl.ds(pl.multiple_of(half * height + peer * SUB, SUB), SUB)
+                copy = pltpu.make_async_remote_copy(
+                    src_ref=back.at[pl.ds(first_pair, count), rows, :],
+                    dst_ref=out_ref.at[pl.ds(first + half * count, count), :, my_cols],
+                    send_sem=out_send.at[2 * g + half, off - 1],
+                    recv_sem=out_recv.at[2 * g + half, off - 1],
+                    device_id=(sec, peer),
+                    device_id_type=MESH,
+                )
+                copy.start()
+                sends.append(copy)
+            own = pl.ds(pl.multiple_of(half * height + dom * SUB, SUB), SUB)
+            out_ref[pl.ds(first + half * count, count), :, my_cols] = back[pl.ds(first_pair, count), own, :]
+
+    a_rows = act_pairs * snaps
+    b_rows = sens_pairs * snaps
+    half_a = lax.broadcasted_iota(jnp.int32, (a_rows, LANES), 1) < height
+
+    def cross_step(index, acc):
+        for part in range(2):
+            lhs, rhs = [], []
+            for side in range(2):
+                base = pl.multiple_of((index * 4 + part * 2 + side) * height_rows, SUB)
+                a = frames[pl.ds(base, a_rows), :]
+                b = frames[pl.ds(base + a_rows, b_rows), :]
+                lhs.append(jnp.concatenate([jnp.where(half_a, a, 0.0), jnp.where(half_a, 0.0, a)], 0).astype(jnp.bfloat16))
+                rhs.append(jnp.concatenate([b, pltpu.roll(b, height, 1)], 0).astype(jnp.bfloat16))
+            acc = acc + lax.dot_general(
+                jnp.concatenate(lhs, 1), jnp.concatenate(rhs, 1), (((1,), (1,)), ((), ())),
+                preferred_element_type=jnp.float32,
+            )
+        return acc
+
+    acc = lax.fori_loop(0, 2 * core // 4, cross_step, jnp.zeros((2 * a_rows, 2 * b_rows), jnp.float32))
+    factor = 1.0 / math.sqrt(height * core * total)
+    acc = acc * factor
+    part_ref[pl.ds(0, a_rows), :] = acc[:a_rows]
+    part_ref[pl.ds(a_rows, a_rows), :] = jnp.concatenate([acc[a_rows:, b_rows:], acc[a_rows:, :b_rows]], 1)
+    for copy in sends:
+        copy.wait()
+
+
+def fast_body(actuator_fields, sensor_fields, region_ids, stiffness_table, density_table, supported):
+    stiffness = lookup(region_ids, stiffness_table)
+    inv_mass = 1.0 / lookup(region_ids, density_table)
+    snaps, _, tiles = supported.shape
+    rows, cols = region_ids.shape
+    mask = jnp.pad(supported[:, 0, :].T.astype(jnp.float32), ((0, 0), (0, LANES - snaps)))
+    mask = jnp.broadcast_to(mask.reshape(1, tiles * LANES), (rows, cols))
+    aux = jnp.stack([stiffness, inv_mass, mask], 0)
+    n_sec, n_dom = lax.axis_size("sec"), lax.axis_size("dom")
+    n_act, n_sens = actuator_fields.shape[0], sensor_fields.shape[0]
+    n_resp = n_act + n_sens
+    pairs = n_resp // 2
+    ext = LANES + 2 * HALO
+    group = 4
+    f32 = jnp.float32
+    vmem = pl.BlockSpec(memory_space=pltpu.VMEM)
+    position, local = pl.pallas_call(
+        functools.partial(wave_kernel, (n_sec, n_dom, n_act, n_sens, 2 * snaps)),
+        out_shape=(
+            jax.ShapeDtypeStruct((n_resp, rows, cols), f32),
+            jax.ShapeDtypeStruct((n_act * snaps, n_sens * snaps), f32),
+        ),
+        in_specs=[vmem] * 3,
+        out_specs=(vmem, vmem),
+        scratch_shapes=[
+            pltpu.VMEM((n_resp + 3, rows * n_dom, LANES), f32),
+            pltpu.VMEM((pairs + 2, ext, LANES), f32),
+            pltpu.VMEM((6, ext, LANES), f32),
+            pltpu.VMEM((16, LANES), f32),
+            pltpu.VMEM((group, ext + 2 * SUB, LANES), f32),
+            pltpu.VMEM((group, ext + 2 * SUB, LANES), f32),
+            pltpu.VMEM((group, ext, LANES), f32),
+            pltpu.VMEM((2 * LANES * pairs * snaps, LANES), f32),
+            pltpu.VMEM((pairs, LANES, LANES), f32),
+            pltpu.SemaphoreType.DMA((3, n_dom - 1)),
+            pltpu.SemaphoreType.DMA((3, n_dom - 1)),
+            pltpu.SemaphoreType.DMA((2,)),
+            pltpu.SemaphoreType.DMA((2,)),
+            pltpu.SemaphoreType.DMA((4, n_dom - 1)),
+            pltpu.SemaphoreType.DMA((4, n_dom - 1)),
+        ],
+        compiler_params=pltpu.CompilerParams(
+            collective_id=0, has_side_effects=True, vmem_limit_bytes=48 * 1024 * 1024
+        ),
+    )(actuator_fields, sensor_fields, aux)
+    total = lax.psum(local, ("sec", "dom"))
+    share = local.shape[0] // n_sec
+    return (position, lax.dynamic_slice_in_dim(total, lax.axis_index("sec") * share, share, 0))
+
+
+def choose(*args):
+    fields, _, region_ids, _, _, supported = args
+    rows, cols = region_ids.shape
+    n_dom = lax.axis_size("dom")
+    fits = (
+        rows == SUB
+        and rows * n_dom * 2 == LANES
+        and cols == LANES * n_dom
+        and 2 * supported.shape[0] <= HALO
+    )
+    return fast_body(*args) if fits else body(*args)
+
+
 def solution(mesh):
     in_specs = (
         P(None, "dom", "sec"),
@@ -107,4 +393,4 @@
         P(None, "dom", "sec"),
     )
     out_specs = (P(None, "dom", "sec"), P("sec", None))
-    return jax.shard_map(body, mesh=mesh, in_specs=in_specs, out_specs=out_specs, check_vma=False)
+    return jax.shard_map(choose, mesh=mesh, in_specs=in_specs, out_specs=out_specs, check_vma=False)

time: 571 us -> 113 us (0.20)
  starting transfers between devices: 251 us -> 0 us
  waiting for transfers between devices: 99.8 us -> 0 us
  other arithmetic: 91.4 us -> 1.66 us
  local copies, waits for them, and re-layouts: 71.5 us -> 2.55 us
  Pallas kernels: 0 us -> 66.6 us
    ppermute x88 -> x0, starting transfers between devices: 251 us -> none  [the longest x44 193 us: padded_2(): lax.ppermute(tail, axis, [(i, (i + 1) % count) for i in range(ends)])]
    ppermute x88 -> x0, waiting for transfers between devices: 99.8 us -> none  [the longest x44 71.7 us: padded_2(): lax.ppermute(tail, axis, [(i, (i + 1) % count) for i in range(ends)])]
    pallas_call x0 -> x1, Pallas kernels: none -> 66.6 us  [fast_body(): pl.pallas_call(functools.partial(wave_kernel, (n_sec, n_dom, n_act, n_sen...]
    add x12 -> x0, other arithmetic: 37.6 us -> none  [the longest x10 36.7 us: advance(): pos_ext = pos_pad[:, 1:-1, 1:-1] + 0.35 * vel_ext]
    slice x50 -> x0, local copies, waits for them, and re-layouts: 37.6 us -> none  [the longest x3 15.9 us: body(): primal = flat_frames[:ACT * SNAPS]]
    mul x62 -> x0, other arithmetic: 27.2 us -> none  [the longest x40 18.9 us: divergence(): total = total + 0.5 * (stiff_centre + stiff_near) * (nearby - centre)]
    concatenate x22 -> x0, local copies, waits for them, and re-layouts: 19.1 us -> none  [padded_2(): jnp.concatenate([lax.ppermute(tail, axis, [(i, (i + 1) % count) for i in...]
    another operation x20 -> x1, other arithmetic: 12 us -> 0.01 us  [fast_body(): aux = jnp.stack([stiffness, inv_mass, mask], 0)]
  transfers between devices with their start and end apart: 88 -> 0, of which waited for: 31 -> 0; matrix products, arithmetic and copies ran while one was open for 12% -> 0% of each run, Pallas kernels for 0% -> 0%
where the time goes in v1:
time: 113 us; the launch traced here: 112 us
  Pallas kernels  66.6 us (59%)
  blocking collectives  40.9 us (36%)
  local copies, waits for them, and re-layouts  2.55 us (2%)
  other arithmetic  1.66 us (1%)
    pallas_call x1, Pallas kernels, fast_body(): pl.pallas_call(functools.partial(wave_kernel, (n_sec, n_dom, n_act, n_sen...  66.6 us
    psum x1, blocking collectives, fast_body(): total = lax.psum(local, ('sec', 'dom'))  40.9 us

profile of v1, /device:TPU:0, one launch (start us, length us, event | category | flops | bytes accessed | tf_op | source)
XLA Modules:
  0.0 112.4 jit_solution(5907533760593436260)
XLA Ops:
  0.6 0.0 copy-start.1
  0.6 1.0 select_reduce_fusion.1
  1.6 0.7 convert_bitcast_fusion
  2.3 0.0 copy-done.1
  2.4 0.0 copy-start
  2.4 1.0 copy-done
  3.4 66.6 %shard_map.77 = (f32[24,8,1024]{2,1,0:T(8,128)S(1)}, f32[160,80]{1,0:T(8,128)S(1)}) custom-call(f32[16,8,1024]{2,1,0:T(8,128)S(1)} %copy-done, f32[8,8,1024]{2,1,0:T(8,128)S(1)} %copy-done.1, f32[3,8,1024]{2,1,0:T(8,128)S(1)} %pad_maximum_fusion.aux_ref), custom_call_target="tpu_custom_call" | custom-call | tf_op jit(solution)/shard_map/pallas_call | solution.py:339
  70.0 40.9 %psum.7 = f32[160,80]{1,0:T(8,128)S(1)} all-reduce(f32[160,80]{1,0:T(8,128)S(1)} %get-tuple-element.5), channel_id=1, replica_groups=mesh['sec'=4,'dom'=8] {'sec','dom'}, use_global_device_ids=true, to_apply=%region_2.3 | all-reduce | flops 12800 | bytes 102400 | tf_op jit(solution)/shard_map/psum | solution.py:368
  110.9 0.6 constant_dynamic-slice_fusion
  111.5 0.9 copy.9
  (4 shorter events, 0.0 us)
Async XLA Ops:
  0.6 1.7 %copy-start.1 = (f32[8,8,1024]{2,1,0:T(8,128)S(1)}, f32[8,8,1024]{2,1,0:T(8,128)}, u32[]{:S(2)}) copy-start(f32[8,8,1024]{2,1,0:T(8,128)} %sens_ref.1) | copy-start | bytes 786436
  2.4 1.0 copy-start

commit v2 on v1

--- a/solution.py
+++ b/solution.py
@@ -106,9 +106,10 @@
 MESH = pl.DeviceIdType.MESH
 
 
-def wave_kernel(dims, act_ref, sens_ref, aux_ref, out_ref, part_ref,
-                recv, field, coef, masks, pos_a, pos_b, vel, frames, back,
-                in_send, in_recv, halo_send, halo_recv, out_send, out_recv):
+def wave_kernel(dims, act_ref, sens_ref, aux_ref, out_ref, cross_ref,
+                recv, field, coef, masks, pos_a, pos_b, vel, frames, back, part, by_sec, by_dom,
+                in_send, in_recv, halo_send, halo_recv, out_send, out_recv,
+                sec_send, sec_recv, dom_send, dom_recv):
     n_sec, n_dom, n_act, n_sens, steps = dims
     sec = lax.axis_index("sec")
     dom = lax.axis_index("dom")
@@ -116,10 +117,14 @@
     total = n_sec * n_dom
     n_resp = n_act + n_sens
     pairs = n_resp // 2
-    act_pairs = n_act // 2
-    sens_pairs = n_sens // 2
+    group = pos_a.shape[0]
+    members = 2 * group
+    groups = n_resp // members
     core = LANES
     ext = core + 2 * HALO
+    height = LANES // 2
+    snaps = steps // 2
+    height_rows = pairs * snaps
     left = lax.rem(place + total - 1, total)
     right = lax.rem(place + 1, total)
     left_id = (left // n_dom, lax.rem(left, n_dom))
@@ -128,69 +133,88 @@
     barrier = pltpu.get_barrier_semaphore()
     for off in range(1, n_dom):
         pl.semaphore_signal(barrier, inc=1, device_id=(sec, lax.rem(dom + off, n_dom)), device_id_type=MESH)
+    for off in range(1, n_sec):
+        pl.semaphore_signal(barrier, inc=1, device_id=(lax.rem(sec + off, n_sec), dom), device_id_type=MESH)
     pl.semaphore_signal(barrier, inc=1, device_id=left_id, device_id_type=MESH)
     pl.semaphore_signal(barrier, inc=1, device_id=right_id, device_id_type=MESH)
-    pl.semaphore_wait(barrier, n_dom + 1)
+    pl.semaphore_wait(barrier, n_dom + n_sec)
 
     my_rows = pl.ds(pl.multiple_of(dom * SUB, SUB), SUB)
     my_cols = pl.ds(pl.multiple_of(dom * LANES, LANES), LANES)
-    groups = ((aux_ref, n_resp, 3), (act_ref, 0, n_act), (sens_ref, n_act, n_sens))
-    copies = []
-    for g, (src, first, count) in enumerate(groups):
+
+    def incoming(src, start, count, first, sem, off):
+        peer = lax.rem(dom + off, n_dom)
+        cols = pl.ds(pl.multiple_of(peer * LANES, LANES), LANES)
+        return pltpu.make_async_remote_copy(
+            src_ref=src.at[pl.ds(start, count), :, cols],
+            dst_ref=recv.at[pl.ds(first, count), my_rows, :],
+            send_sem=in_send.at[sem, off - 1],
+            recv_sem=in_recv.at[sem, off - 1],
+            device_id=(sec, peer),
+            device_id_type=MESH,
+        )
+
+    sources = [(aux_ref, 0, 3, n_resp, groups)]
+    for g in range(groups):
+        at = g * members
+        src, start = (act_ref, at) if at < n_act else (sens_ref, at - n_act)
+        sources.append((src, start, members, at, g))
+    arrivals = []
+    for src, start, count, first, sem in sources:
         for off in range(1, n_dom):
-            peer = lax.rem(dom + off, n_dom)
-            cols = pl.ds(pl.multiple_of(peer * LANES, LANES), LANES)
-            copy = pltpu.make_async_remote_copy(
-                src_ref=src.at[:, :, cols],
-                dst_ref=recv.at[pl.ds(first, count), my_rows, :],
-                send_sem=in_send.at[g, off - 1],
-                recv_sem=in_recv.at[g, off - 1],
-                device_id=(sec, peer),
-                device_id_type=MESH,
-            )
+            copy = incoming(src, start, count, first, sem, off)
             copy.start()
-            copies.append(copy)
-    for src, first, count in groups:
-        recv[pl.ds(first, count), my_rows, :] = src[:, :, my_cols]
-    for copy in copies:
-        copy.wait()
+            arrivals.append(copy)
+    for src, start, count, first, sem in sources:
+        recv[pl.ds(first, count), my_rows, :] = src[pl.ds(start, count), :, my_cols]
 
     inner = pl.ds(HALO, core)
+
+    def halo(count, first, sem):
+        to_left = pltpu.make_async_remote_copy(
+            src_ref=field.at[pl.ds(first, count), pl.ds(HALO, HALO), :],
+            dst_ref=field.at[pl.ds(first, count), pl.ds(HALO + core, HALO), :],
+            send_sem=halo_send.at[sem, 0], recv_sem=halo_recv.at[sem, 0],
+            device_id=left_id, device_id_type=MESH,
+        )
+        to_right = pltpu.make_async_remote_copy(
+            src_ref=field.at[pl.ds(first, count), pl.ds(core, HALO), :],
+            dst_ref=field.at[pl.ds(first, count), pl.ds(0, HALO), :],
+            send_sem=halo_send.at[sem, 1], recv_sem=halo_recv.at[sem, 1],
+            device_id=right_id, device_id_type=MESH,
+        )
+        return to_left, to_right
+
+    def group_halo(g):
+        return halo(group, g * group, g)
+
+    def aux_halo():
+        return halo(2, pairs, groups)
 
     def flip(first, second):
         return jnp.concatenate([recv[first], recv[second]], 0).T
 
-    for p in range(pairs):
-        if p < act_pairs:
-            first, second = p, p + act_pairs
-        else:
-            first = n_act + p - act_pairs
-            second = first + sens_pairs
-        field[p, inner, :] = flip(first, second)
+    def receive_group(g):
+        for off in range(1, n_dom):
+            incoming(act_ref, 0, members, g * members, g, off).wait_recv()
+        for q in range(group):
+            field[g * group + q, inner, :] = flip(g * members + q, g * members + group + q)
+        for copy in group_halo(g):
+            copy.start()
+
+    for copy in arrivals[: n_dom - 1]:
+        copy.wait_recv()
     field[pairs, inner, :] = flip(n_resp, n_resp)
     field[pairs + 1, inner, :] = flip(n_resp + 1, n_resp + 1)
     masks[...] = flip(n_resp + 2, n_resp + 2)[: masks.shape[0], :]
-
-    to_left = pltpu.make_async_remote_copy(
-        src_ref=field.at[:, pl.ds(HALO, HALO), :],
-        dst_ref=field.at[:, pl.ds(HALO + core, HALO), :],
-        send_sem=halo_send.at[0], recv_sem=halo_recv.at[0],
-        device_id=left_id, device_id_type=MESH,
-    )
-    to_right = pltpu.make_async_remote_copy(
-        src_ref=field.at[:, pl.ds(core, HALO), :],
-        dst_ref=field.at[:, pl.ds(0, HALO), :],
-        send_sem=halo_send.at[1], recv_sem=halo_recv.at[1],
-        device_id=right_id, device_id_type=MESH,
-    )
-    to_left.start()
-    to_right.start()
-    to_left.wait()
-    to_right.wait()
+    for copy in aux_halo():
+        copy.start()
+    receive_group(0)
+    for copy in aux_halo():
+        copy.wait()
 
     where = lax.broadcasted_iota(jnp.int32, (ext, LANES), 0)
     lane = lax.broadcasted_iota(jnp.int32, (ext, LANES), 1)
-    height = LANES // 2
     row = lax.rem(lane, height)
     low = jnp.where(place == 0, HALO, 0)
     high = jnp.where(place == total - 1, HALO + core, ext)
@@ -216,12 +240,10 @@
     coef[5] = 0.35 * mass
 
     n_tiles = ext // SUB
-    group = pos_a.shape[0]
-    snaps = steps // 2
-    height_rows = pairs * snaps
-
-    def advance(src, dst, store):
-        for t in range(n_tiles):
+    halo_tiles = HALO // SUB
+
+    def advance(src, dst, skip, store):
+        for t in range(skip, n_tiles - skip):
             at = pl.ds(t * SUB, SUB)
             cs = [coef[c, at, :] for c in range(5)]
             for q in range(group):
@@ -243,64 +265,82 @@
         buf[:, pl.ds(0, SUB), :] = pad
         buf[:, pl.ds(SUB + ext, SUB), :] = pad
 
-    def run_group(index, carry):
+    def outgoing(g, off):
+        peer = lax.rem(dom + off, n_dom)
+        rows = pl.ds(pl.multiple_of(peer * SUB, SUB), SUB)
+        planes = pl.ds(g * members, members)
+        return pltpu.make_async_remote_copy(
+            src_ref=back.at[planes, rows, :],
+            dst_ref=out_ref.at[planes, :, my_cols],
+            send_sem=out_send.at[g, off - 1],
+            recv_sem=out_recv.at[g, off - 1],
+            device_id=(sec, peer),
+            device_id_type=MESH,
+        )
+
+    def run_group(g, carry):
+        for copy in group_halo(g):
+            copy.wait()
+
+        @pl.when(g < groups - 1)
+        def _():
+            receive_group(g + 1)
+
         for q in range(group):
-            here = index * group + q
-            vel[q] = jnp.where(inside, field[here] * coef[5], 0.0)
-            pos_a[q, pl.ds(SUB, ext), :] = jnp.zeros((ext, LANES), jnp.float32)
-
-        def pair_step(k, carry):
+            start = jnp.where(inside, field[g * group + q] * coef[5], 0.0)
+            vel[q] = start
+            pos_b[q, pl.ds(SUB, ext), :] = start
+
+        def half_step(k, skip):
             mask = jnp.broadcast_to(masks[pl.ds(k, 1), :], (SUB, LANES))
             vmask = mask * (1.0 / 0.35)
 
             def store(q, t, new_pos, new_vel):
-                if t * SUB < HALO or t * SUB >= HALO + core:
+                if t < halo_tiles or t >= n_tiles - halo_tiles:
                     return
-                y = t * SUB - HALO
-                base = y * height_rows + (index * group + q) * snaps + k
+                y = (t - halo_tiles) * SUB
+                base = y * height_rows + (g * group + q) * snaps + k
                 frames[pl.ds(base, SUB, stride=height_rows), :] = new_pos * mask
                 frames[pl.ds(base + core * height_rows, SUB, stride=height_rows), :] = new_vel * vmask
 
-            advance(pos_a, pos_b, None)
-            advance(pos_b, pos_a, store)
-            return carry
-
-        lax.fori_loop(0, snaps, pair_step, 0)
+            advance(pos_b, pos_a, skip, store)
+
+        half_step(0, 0)
+        first = 1
+        for skip in range(halo_tiles):
+            last = first
+            while last < snaps and (steps - 2 * last - 1 > (halo_tiles - 1 - skip) * SUB or skip == halo_tiles - 1):
+                last += 1
+
+            def pair_step(k, carry, skip=skip):
+                advance(pos_a, pos_b, skip, None)
+                half_step(k, skip)
+                return carry
+
+            if last > first:
+                lax.fori_loop(first, last, pair_step, 0)
+            first = last
         for q in range(group):
-            back[index * group + q] = pos_a[q, pl.ds(SUB + HALO, core), :].T
+            turned = pos_a[q, pl.ds(SUB + HALO, core), :].T
+            back[g * members + q] = turned[:height]
+            back[g * members + group + q] = turned[height:]
+        for off in range(1, n_dom):
+            outgoing(g, off).start()
         return carry
 
-    lax.fori_loop(0, pairs // group, run_group, 0)
-
-    sends = []
-    parts = ((0, act_pairs, 0), (act_pairs, sens_pairs, n_act))
-    for g, (first_pair, count, first) in enumerate(parts):
-        for half in range(2):
-            for off in range(1, n_dom):
-                peer = lax.rem(dom + off, n_dom)
-                rows = pl.ds(pl.multiple_of(half * height + peer * SUB, SUB), SUB)
-                copy = pltpu.make_async_remote_copy(
-                    src_ref=back.at[pl.ds(first_pair, count), rows, :],
-                    dst_ref=out_ref.at[pl.ds(first + half * count, count), :, my_cols],
-                    send_sem=out_send.at[2 * g + half, off - 1],
-                    recv_sem=out_recv.at[2 * g + half, off - 1],
-                    device_id=(sec, peer),
-                    device_id_type=MESH,
-                )
-                copy.start()
-                sends.append(copy)
-            own = pl.ds(pl.multiple_of(half * height + dom * SUB, SUB), SUB)
-            out_ref[pl.ds(first + half * count, count), :, my_cols] = back[pl.ds(first_pair, count), own, :]
-
-    a_rows = act_pairs * snaps
-    b_rows = sens_pairs * snaps
+    lax.fori_loop(0, groups, run_group, 0)
+    out_ref[:, :, my_cols] = back[:, my_rows, :]
+
+    a_pairs = n_act // 2
+    a_rows = a_pairs * snaps
+    b_rows = (pairs - a_pairs) * snaps
     half_a = lax.broadcasted_iota(jnp.int32, (a_rows, LANES), 1) < height
 
     def cross_step(index, acc):
-        for part in range(2):
+        for piece in range(2):
             lhs, rhs = [], []
             for side in range(2):
-                base = pl.multiple_of((index * 4 + part * 2 + side) * height_rows, SUB)
+                base = pl.multiple_of((index * 4 + piece * 2 + side) * height_rows, SUB)
                 a = frames[pl.ds(base, a_rows), :]
                 b = frames[pl.ds(base + a_rows, b_rows), :]
                 lhs.append(jnp.concatenate([jnp.where(half_a, a, 0.0), jnp.where(half_a, 0.0, a)], 0).astype(jnp.bfloat16))
@@ -312,12 +352,50 @@
         return acc
 
     acc = lax.fori_loop(0, 2 * core // 4, cross_step, jnp.zeros((2 * a_rows, 2 * b_rows), jnp.float32))
-    factor = 1.0 / math.sqrt(height * core * total)
-    acc = acc * factor
-    part_ref[pl.ds(0, a_rows), :] = acc[:a_rows]
-    part_ref[pl.ds(a_rows, a_rows), :] = jnp.concatenate([acc[a_rows:, b_rows:], acc[a_rows:, :b_rows]], 1)
-    for copy in sends:
+    second = jnp.concatenate([acc[a_rows:, b_rows:], acc[a_rows:, :b_rows]], 1)
+    share = group * snaps
+    for g in range(n_act // members):
+        part[2 * g] = acc[g * share : (g + 1) * share]
+        part[2 * g + 1] = second[g * share : (g + 1) * share]
+
+    swaps = []
+    for off in range(1, n_sec):
+        peer = lax.rem(sec + off, n_sec)
+        copy = pltpu.make_async_remote_copy(
+            src_ref=part.at[peer], dst_ref=by_sec.at[sec],
+            send_sem=sec_send.at[off - 1], recv_sem=sec_recv.at[off - 1],
+            device_id=(peer, dom), device_id_type=MESH,
+        )
+        copy.start()
+        swaps.append(copy)
+    by_sec[sec] = part[sec]
+    for copy in swaps:
         copy.wait()
+    value = by_sec[0]
+    for s in range(1, n_sec):
+        value = value + by_sec[s]
+    by_dom[dom] = value
+    swaps = []
+    for off in range(1, n_dom):
+        copy = pltpu.make_async_remote_copy(
+            src_ref=by_dom.at[dom], dst_ref=by_dom.at[dom],
+            send_sem=dom_send.at[off - 1], recv_sem=dom_recv.at[off - 1],
+            device_id=(sec, lax.rem(dom + off, n_dom)), device_id_type=MESH,
+        )
+        copy.start()
+        swaps.append(copy)
+    for copy in swaps:
+        copy.wait()
+    value = by_dom[0]
+    for d in range(1, n_dom):
+        value = value + by_dom[d]
+    cross_ref[...] = value * (1.0 / math.sqrt(height * core * total))
+
+    for copy in arrivals:
+        copy.wait_send()
+    for g in range(groups):
+        for off in range(1, n_dom):
+            outgoing(g, off).wait()
 
 
 def fast_body(actuator_fields, sensor_fields, region_ids, stiffness_table, density_table, supported):
@@ -336,11 +414,15 @@
     group = 4
     f32 = jnp.float32
     vmem = pl.BlockSpec(memory_space=pltpu.VMEM)
-    position, local = pl.pallas_call(
+    groups = pairs // group
+    share = n_act * snaps // n_sec
+    piece = (share, n_sens * snaps)
+    sem = pltpu.SemaphoreType.DMA
+    return pl.pallas_call(
         functools.partial(wave_kernel, (n_sec, n_dom, n_act, n_sens, 2 * snaps)),
         out_shape=(
             jax.ShapeDtypeStruct((n_resp, rows, cols), f32),
-            jax.ShapeDtypeStruct((n_act * snaps, n_sens * snaps), f32),
+            jax.ShapeDtypeStruct(piece, f32),
         ),
         in_specs=[vmem] * 3,
         out_specs=(vmem, vmem),
@@ -353,25 +435,29 @@
             pltpu.VMEM((group, ext + 2 * SUB, LANES), f32),
             pltpu.VMEM((group, ext, LANES), f32),
             pltpu.VMEM((2 * LANES * pairs * snaps, LANES), f32),
-            pltpu.VMEM((pairs, LANES, LANES), f32),
-            pltpu.SemaphoreType.DMA((3, n_dom - 1)),
-            pltpu.SemaphoreType.DMA((3, n_dom - 1)),
-            pltpu.SemaphoreType.DMA((2,)),
-            pltpu.SemaphoreType.DMA((2,)),
-            pltpu.SemaphoreType.DMA((4, n_dom - 1)),
-            pltpu.SemaphoreType.DMA((4, n_dom - 1)),
+            pltpu.VMEM((n_resp, rows * n_dom, LANES), f32),
+            pltpu.VMEM((n_sec, *piece), f32),
+            pltpu.VMEM((n_sec, *piece), f32),
+            pltpu.VMEM((n_dom, *piece), f32),
+            sem((groups + 1, n_dom - 1)),
+            sem((groups + 1, n_dom - 1)),
+            sem((groups + 1, 2)),
+            sem((groups + 1, 2)),
+            sem((groups, n_dom - 1)),
+            sem((groups, n_dom - 1)),
+            sem((n_sec - 1,)),
+            sem((n_sec - 1,)),
+            sem((n_dom - 1,)),
+            sem((n_dom - 1,)),
         ],
         compiler_params=pltpu.CompilerParams(
             collective_id=0, has_side_effects=True, vmem_limit_bytes=48 * 1024 * 1024
         ),
     )(actuator_fields, sensor_fields, aux)
-    total = lax.psum(local, ("sec", "dom"))
-    share = local.shape[0] // n_sec
-    return (position, lax.dynamic_slice_in_dim(total, lax.axis_index("sec") * share, share, 0))
 
 
 def choose(*args):
-    fields, _, region_ids, _, _, supported = args
+    fields, sensors, region_ids, _, _, supported = args
     rows, cols = region_ids.shape
     n_dom = lax.axis_size("dom")
     fits = (
@@ -379,6 +465,9 @@
         and rows * n_dom * 2 == LANES
         and cols == LANES * n_dom
         and 2 * supported.shape[0] <= HALO
+        and fields.shape[0] == 4 * lax.axis_size("sec")
+        and fields.shape[0] % 8 == 0
+        and sensors.shape[0] == 8
     )
     return fast_body(*args) if fits else body(*args)
 

time: 113 us -> 77.7 us (0.69)
  blocking collectives: 40.9 us -> 0 us
  Pallas kernels: 66.6 us -> 72.7 us
    psum x1 -> x0, blocking collectives: 40.9 us -> none  [fast_body(): total = lax.psum(local, ('sec', 'dom'))]
    pallas_call x1, Pallas kernels: 66.6 us -> 72.7 us  [fast_body(): pl.pallas_call(functools.partial(wave_kernel, (n_sec, n_dom, n_act, n_sen...]
    unnamed x5 -> x8, local copies, waits for them, and re-layouts: 1.92 us -> 2.53 us
where the time goes in v2:
time: 77.7 us; the launch traced here: 77.5 us
  Pallas kernels  72.7 us (94%)
  local copies, waits for them, and re-layouts  2.55 us (3%)
  other arithmetic  1.58 us (2%)
    pallas_call x1, Pallas kernels, fast_body(): pl.pallas_call(functools.partial(wave_kernel, (n_sec, n_dom, n_act, n_sen...  72.7 us
    unnamed x8, local copies, waits for them, and re-layouts  2.53 us

profile of v2, /device:TPU:0, one launch (start us, length us, event | category | flops | bytes accessed | tf_op | source)
XLA Modules:
  0.0 77.5 jit_solution(10093941349692322579)
XLA Ops:
  0.6 0.0 copy-start.2
  0.6 0.0 copy-start.1
  0.7 0.7 convert_bitcast_fusion
  1.4 0.0 copy-done.2
  1.4 0.8 %select_reduce_fusion.1 = (f32[8,1024]{1,0:T(8,128)S(1)}, f32[8,1024]{1,0:T(8,128)S(1)}) fusion(f32[16]{0:T(128)} %param.9, s32[8,1024]{1,0:T(8,128)S(1)} %copy-done.2, f32[16]{0:T(128)} %param.10), kind=kLoop, calls=%fused_computation.1 | loop fusion | flops 638976 | bytes 98432 | tf_op jit(solution)/shard_map/reduce_sum | solution.py:49
  2.3 0.0 copy-done.1
  2.3 0.0 copy-start
  2.3 1.0 %copy-done = f32[16,8,1024]{2,1,0:T(8,128)S(1)} copy-done((f32[16,8,1024]{2,1,0:T(8,128)S(1)}, f32[16,8,1024]{2,1,0:T(8,128)}, u32[]{:S(2)}) %copy-start) | copy-done | bytes 524312
  3.3 72.7 %shard_map.77 = (f32[24,8,1024]{2,1,0:T(8,128)S(1)}, f32[40,80]{1,0:T(8,128)S(1)}) custom-call(f32[16,8,1024]{2,1,0:T(8,128)S(1)} %copy-done, f32[8,8,1024]{2,1,0:T(8,128)S(1)} %copy-done.1, f32[3,8,1024]{2,1,0:T(8,128)S(1)} %pad_maximum_fusion.aux_ref), custom_call_target="tpu_custom_call" | custom-call | tf_op jit(solution)/shard_map/pallas_call | solution.py:421
  76.0 0.9 %copy.10 = f32[24,8,1024]{2,1,0:T(8,128)} copy(f32[24,8,1024]{2,1,0:T(8,128)S(1)} %get-tuple-element.6) | data formatting | bytes 1572864
  76.9 0.6 copy.11
  (4 shorter events, 0.0 us)
Async XLA Ops:
  0.6 0.8 copy-start.2
  0.6 1.6 %copy-start.1 = (f32[8,8,1024]{2,1,0:T(8,128)S(1)}, f32[8,8,1024]{2,1,0:T(8,128)}, u32[]{:S(2)}) copy-start(f32[8,8,1024]{2,1,0:T(8,128)} %sens_ref.1) | copy-start | bytes 786436
  2.3 1.0 %copy-start = (f32[16,8,1024]{2,1,0:T(8,128)S(1)}, f32[16,8,1024]{2,1,0:T(8,128)}, u32[]{:S(2)}) copy-start(f32[16,8,1024]{2,1,0:T(8,128)} %act_ref.1) | copy-start | bytes 1572868

commit v3 on v2

--- a/solution.py
+++ b/solution.py
@@ -282,10 +282,6 @@
         for copy in group_halo(g):
             copy.wait()
 
-        @pl.when(g < groups - 1)
-        def _():
-            receive_group(g + 1)
-
         for q in range(group):
             start = jnp.where(inside, field[g * group + q] * coef[5], 0.0)
             vel[q] = start
@@ -320,6 +316,12 @@
             if last > first:
                 lax.fori_loop(first, last, pair_step, 0)
             first = last
+            if skip == 1:
+
+                @pl.when(g < groups - 1)
+                def _():
+                    receive_group(g + 1)
+
         for q in range(group):
             turned = pos_a[q, pl.ds(SUB + HALO, core), :].T
             back[g * members + q] = turned[:height]
@@ -336,27 +338,31 @@
     b_rows = (pairs - a_pairs) * snaps
     half_a = lax.broadcasted_iota(jnp.int32, (a_rows, LANES), 1) < height
 
+    chunk = 32
+
     def cross_step(index, acc):
-        for piece in range(2):
-            lhs, rhs = [], []
-            for side in range(2):
-                base = pl.multiple_of((index * 4 + piece * 2 + side) * height_rows, SUB)
-                a = frames[pl.ds(base, a_rows), :]
-                b = frames[pl.ds(base + a_rows, b_rows), :]
-                lhs.append(jnp.concatenate([jnp.where(half_a, a, 0.0), jnp.where(half_a, 0.0, a)], 0).astype(jnp.bfloat16))
-                rhs.append(jnp.concatenate([b, pltpu.roll(b, height, 1)], 0).astype(jnp.bfloat16))
-            acc = acc + lax.dot_general(
-                jnp.concatenate(lhs, 1), jnp.concatenate(rhs, 1), (((1,), (1,)), ((), ())),
-                preferred_element_type=jnp.float32,
-            )
-        return acc
-
-    acc = lax.fori_loop(0, 2 * core // 4, cross_step, jnp.zeros((2 * a_rows, 2 * b_rows), jnp.float32))
+        lhs, rhs = [], []
+        for side in range(chunk):
+            base = pl.multiple_of((index * chunk + side) * height_rows, SUB)
+            a = frames[pl.ds(base, a_rows), :]
+            b = frames[pl.ds(base + a_rows, b_rows), :]
+            lhs.append(jnp.concatenate([jnp.where(half_a, a, 0.0), jnp.where(half_a, 0.0, a)], 0).astype(jnp.bfloat16))
+            rhs.append(jnp.concatenate([b, pltpu.roll(b, height, 1)], 0).astype(jnp.bfloat16))
+        return acc + lax.dot_general(
+            jnp.concatenate(lhs, 1), jnp.concatenate(rhs, 1), (((1,), (1,)), ((), ())),
+            preferred_element_type=jnp.float32,
+        )
+
+    acc = lax.fori_loop(0, 2 * core // chunk, cross_step, jnp.zeros((2 * a_rows, 2 * b_rows), jnp.float32))
     second = jnp.concatenate([acc[a_rows:, b_rows:], acc[a_rows:, :b_rows]], 1)
-    share = group * snaps
+    ordered = []
     for g in range(n_act // members):
-        part[2 * g] = acc[g * share : (g + 1) * share]
-        part[2 * g + 1] = second[g * share : (g + 1) * share]
+        rows = slice(g * group * snaps, (g + 1) * group * snaps)
+        ordered += [acc[rows], second[rows]]
+    ordered = jnp.concatenate(ordered, 0)
+    share = part.shape[1]
+    for s in range(n_sec):
+        part[s] = ordered[s * share : (s + 1) * share]
 
     swaps = []
     for off in range(1, n_sec):
@@ -389,7 +395,12 @@
     value = by_dom[0]
     for d in range(1, n_dom):
         value = value + by_dom[d]
-    cross_ref[...] = value * (1.0 / math.sqrt(height * core * total))
+    value = value * (1.0 / math.sqrt(height * core * total))
+    wide = group * snaps
+    order = [
+        value[:, h * b_rows + g * wide : h * b_rows + (g + 1) * wide] for g in range(n_sens // members) for h in range(2)
+    ]
+    cross_ref[...] = jnp.concatenate(order, 1)
 
     for copy in arrivals:
         copy.wait_send()

time: 77.7 us -> 64.3 us (0.83)
  Pallas kernels: 72.7 us -> 59.3 us
    pallas_call x1, Pallas kernels: 72.7 us -> 59.3 us  [fast_body(): pl.pallas_call(functools.partial(wave_kernel, (n_sec, n_dom, n_act, n_sen...]
where the time goes in v3:
time: 64.3 us; the launch traced here: 64.1 us
  Pallas kernels  59.3 us (92%)
  local copies, waits for them, and re-layouts  2.55 us (4%)
  other arithmetic  1.58 us (2%)
  between operations  0.7 us (1%)
    pallas_call x1, Pallas kernels, fast_body(): pl.pallas_call(functools.partial(wave_kernel, (n_sec, n_dom, n_act, n_sen...  59.3 us
    unnamed x8, local copies, waits for them, and re-layouts  2.53 us

profile of v3, /device:TPU:0, one launch (start us, length us, event | category | flops | bytes accessed | tf_op | source)
XLA Modules:
  0.0 64.1 jit_solution(10637553341608988351)
XLA Ops:
  0.6 0.0 copy-start.2
  0.6 0.0 copy-start.1
  0.7 0.7 %convert_bitcast_fusion = f32[8,10]{1,0:T(8,128)S(1)} fusion(s32[10,1,8]{0,2,1:T(8,128)} %param.11), kind=kLoop, calls=%fused_computation.6 | loop fusion | flops 80 | bytes 640 | tf_op jit(solution)/shard_map/convert_element_type | solution.py:417
  1.4 0.0 copy-done.2
  1.4 0.8 %select_reduce_fusion.1 = (f32[8,1024]{1,0:T(8,128)S(1)}, f32[8,1024]{1,0:T(8,128)S(1)}) fusion(f32[16]{0:T(128)} %param.9, s32[8,1024]{1,0:T(8,128)S(1)} %copy-done.2, f32[16]{0:T(128)} %param.10), kind=kLoop, calls=%fused_computation.1 | loop fusion | flops 638976 | bytes 98432 | tf_op jit(solution)/shard_map/reduce_sum | solution.py:49
  2.3 0.0 copy-done.1
  2.3 0.0 copy-start
  2.3 1.0 %copy-done = f32[16,8,1024]{2,1,0:T(8,128)S(1)} copy-done((f32[16,8,1024]{2,1,0:T(8,128)S(1)}, f32[16,8,1024]{2,1,0:T(8,128)}, u32[]{:S(2)}) %copy-start) | copy-done | bytes 524312
  3.3 59.3 %shard_map.77 = (f32[24,8,1024]{2,1,0:T(8,128)S(1)}, f32[40,80]{1,0:T(8,128)S(1)}) custom-call(f32[16,8,1024]{2,1,0:T(8,128)S(1)} %copy-done, f32[8,8,1024]{2,1,0:T(8,128)S(1)} %copy-done.1, f32[3,8,1024]{2,1,0:T(8,128)S(1)} %pad_maximum_fusion.aux_ref), custom_call_target="tpu_custom_call" | custom-call | tf_op jit(solution)/shard_map/pallas_call | solution.py:432
  62.6 0.9 %copy.10 = f32[24,8,1024]{2,1,0:T(8,128)} copy(f32[24,8,1024]{2,1,0:T(8,128)S(1)} %get-tuple-element.6) | data formatting | bytes 1572864
  63.5 0.6 copy.11
  (4 shorter events, 0.0 us)
Async XLA Ops:
  0.6 0.8 %copy-start.2 = (s32[8,1024]{1,0:T(8,128)S(1)}, s32[8,1024]{1,0:T(8,128)}, u32[]{:S(2)}) copy-start(s32[8,1024]{1,0:T(8,128)} %param.8) | copy-start | bytes 98308
  0.6 1.6 %copy-start.1 = (f32[8,8,1024]{2,1,0:T(8,128)S(1)}, f32[8,8,1024]{2,1,0:T(8,128)}, u32[]{:S(2)}) copy-start(f32[8,8,1024]{2,1,0:T(8,128)} %sens_ref.1) | copy-start | bytes 786436
  2.3 1.0 %copy-start = (f32[16,8,1024]{2,1,0:T(8,128)S(1)}, f32[16,8,1024]{2,1,0:T(8,128)}, u32[]{:S(2)}) copy-start(f32[16,8,1024]{2,1,0:T(8,128)} %act_ref.1) | copy-start | bytes 1572868
